TPU v7x, 32 devices: a whole 2x2x4 slice. The times are simulated.
32 devices in a mesh: views: 8 (over y, x, core), rows: 4 (over z).
Axes of the slice: x: 2, y: 2, z: 4, core: 2. Of those that a mesh axis runs over, the one named last changes fastest.
Arguments:
- projections: float32 [128, 8, 4096], P('views', 'rows'), may hold values from 0.0002 to 1.2, as said below
- partner: int32 [64], replicated, may hold values from 64 to 127, as said below
- geometry: int32 [2, 8], replicated, may hold values from 0 to 512, as said below
Outputs:
- sinogram: float32 [64, 8, 7680], P('views', 'rows')
Inputs may be any that keep to these rules, and one draw needn't show every extreme that they name: Each value appears once, and partner[j] - 64 lies in the same aligned block of 16 views as j. geometry[0, r] lies between 256 and 512; geometry[1, r] lies between 0 and 512 - geometry[0, r]. `projections`: positive transmissions.
All inputs are finite; a program needn't handle non-finite values.
Results may differ from a plain program's by a relative error of at most 0.0003.
Values sent between devices are 32-bit elements; how exact they have to be, the bound alone decides.
A program may use at most 64 MiB of HBM per device.

v0:
```python
import functools
import math

import jax
import jax.numpy as jnp
import numpy as np
from jax import lax
from jax.experimental import pallas as pl
from jax.experimental.pallas import tpu as pltpu
from jax.sharding import PartitionSpec as P

GBAND = 4
WIDE = 7680
LANES = 128
TURNS = WIDE // LANES
PAD = 32
NCOEF = 2 * GBAND - 1
SLOT = 8

SHRINK_FLOOR = 1e-06
MESH = pl.DeviceIdType.MESH


def each(count, body):
    if count <= 16:
        for i in range(count):
            body(i)
    else:
        lax.fori_loop(0, count, lambda i, c: (body(i), c)[1], 0)


def split_np(table):
    hi = np.asarray(table, np.float32).astype(jnp.bfloat16)
    lo = (np.asarray(table, np.float64) - hi.astype(np.float64)).astype(jnp.bfloat16)
    return hi, lo


def split(x):
    hi = x.astype(jnp.bfloat16)
    lo = (x - hi.astype(jnp.float32)).astype(jnp.bfloat16)
    return hi, lo


def phase_table():
    i = np.arange(LANES)[:, None]
    j = np.arange(LANES)[None, :]
    parts = []
    for apart in (0, 1, -1):
        dist = np.abs(LANES * apart + j - i)
        parts.append(np.where(dist <= 126, np.exp2(-np.minimum(dist, 126).astype(np.float64)), 0.0))
    one = np.concatenate(parts, axis=1)
    return np.stack([one, one[::-1]]).astype(jnp.bfloat16)


def ramp_tables(left_blocks, right_start):
    k = np.arange(PAD)
    a = np.concatenate([np.arange(left_blocks), right_start + np.arange(left_blocks)])
    live = (k <= TURNS // 2)[:, None]
    ang = 2.0 * math.pi / TURNS * ((k[:, None] * a[None, :]) % TURNS)
    first = np.concatenate([np.where(live, np.cos(ang), 0), np.where(live, -np.sin(ang), 0)])
    fhi, flo = split_np(first)
    first = np.concatenate([fhi, fhi, flo], axis=1)
    b = np.arange(LANES)
    ang = 2.0 * math.pi / LANES * ((b[:, None] * b[None, :]) % LANES)
    c, s = np.cos(ang), np.sin(ang)
    fwd = split_np(np.block([[c, -s], [s, c]]))
    inv = split_np(np.block([[c, s], [-s, c]]))
    ang = 2.0 * math.pi / WIDE * ((k[:, None] * b[None, :]) % WIDE)
    twist = np.stack([np.cos(ang), np.sin(ang)]).astype(np.float32)
    freq = TURNS * b[None, :] + k[:, None]
    times = np.where((k == 0) | (k == TURNS // 2), 1.0, 2.0)[:, None]
    response = np.where(live, 2.0 * np.minimum(freq, WIDE - freq) / WIDE * times / WIDE, 0.0)
    a = np.arange(64)
    ang = 2.0 * math.pi / TURNS * ((a[:, None] * k[None, :]) % TURNS)
    last = np.concatenate([np.cos(ang), -np.sin(ang)], axis=1) * np.concatenate([live, live])[:, 0]
    lhi, llo = split_np(last)
    last = np.concatenate([lhi, lhi, llo], axis=1)
    return first, np.stack(fwd), np.stack(inv), twist, response.astype(np.float32), last


def band_tables(half_total):
    j = np.arange(half_total)[:, None]
    g = np.arange(GBAND)[None, :]
    ang = 2.0 * math.pi / half_total * ((j * g) % half_total)
    zero = np.zeros((half_total, 1))
    fwd = np.concatenate([np.cos(ang), -np.sin(ang[:, 1:]), zero], axis=1)
    dbl = np.where(g == 0, 1.0, 2.0)
    inv = np.concatenate([dbl * np.cos(ang), -2.0 * np.sin(ang[:, 1:]), zero], axis=1) / half_total
    return np.concatenate([fwd, inv], axis=1).reshape(-1).astype(np.float32)


def dot(a, b):
    return jnp.dot(a, b, preferred_element_type=jnp.float32)


def kernel(
    n, nr, views, blocks, rows_total,
    partner, geometry, band, x_ref, phase_ref, first_ref, fwd_ref, inv_ref, twist_ref, resp_ref, last_ref,
    out_ref,
    st, cbuf, rsbuf, agbuf, full, pwbuf, mid, mv, z,
    ex_send, ex_recv, rs_send, rs_recv, ag_send, ag_recv, pw_send, pw_recv,
):
    half = n // 2
    paired = views // 2
    me = lax.axis_index("views")
    my_row = lax.axis_index("rows")
    upper = me >= half
    up = jnp.where(upper, 1, 0)
    s = lax.rem(me, half)
    side = 1 - up
    other = lax.rem(me + half, n)
    strip = cbuf.shape[0] // half
    cols = blocks * LANES
    vrows = 2 * blocks

    barrier = pltpu.get_barrier_semaphore()

    def greet_view(d):
        pl.semaphore_signal(barrier, inc=1, device_id={"views": lax.rem(me + d + 1, n)}, device_id_type=MESH)

    def greet_row(d):
        pl.semaphore_signal(barrier, inc=1, device_id={"rows": lax.rem(my_row + d + 1, nr)}, device_id_type=MESH)

    each(n - 1, greet_view)
    each(nr - 1, greet_row)

    margins = [geometry[0, my_row * 2 + r] for r in range(2)]
    offsets = [geometry[1, my_row * 2 + r] for r in range(2)]
    move = [jnp.where(upper, cols - offsets[r], 2 * cols - WIDE - margins[r] - offsets[r]) for r in range(2)]
    whole = [move[r] // LANES for r in range(2)]
    rest = [move[r] - whole[r] * LANES for r in range(2)]
    ri = lax.broadcasted_iota(jnp.int32, (vrows, vrows), 0)
    ci = lax.broadcasted_iota(jnp.int32, (vrows, vrows), 1)
    second = ri >= blocks
    a_id = jnp.where(second, ri - blocks, ri)
    a_id = a_id - jnp.where(second, whole[1], whole[0])
    a_id = jnp.where(a_id < 0, a_id + blocks, a_id)
    a_id = jnp.where(upper, blocks - 1 - a_id, a_id)
    pick = (ci == 2 * a_id + jnp.where(second, 1, 0)).astype(jnp.float32).astype(jnp.bfloat16)

    rl = lax.broadcasted_iota(jnp.int32, (vrows, LANES), 0)
    lane = lax.broadcasted_iota(jnp.int32, (vrows, LANES), 1)
    sec = rl >= blocks
    t = jnp.where(sec, rl - blocks, rl) * LANES + lane + jnp.where(upper, 0, WIDE - cols)
    offs = jnp.where(sec, offsets[1], offsets[0])
    marg = jnp.where(sec, margins[1], margins[0])
    ramp = ((t + offs - cols + marg).astype(jnp.float32) + 0.5) / marg.astype(jnp.float32)
    w = jnp.minimum(jnp.maximum(ramp, 0.0), 1.0)
    weight = jnp.where(upper, 1.0 - w, w)
    lane_b = lax.broadcasted_iota(jnp.int32, (blocks, LANES), 1)

    half_total = views * half
    base = s * views
    r128 = lax.broadcasted_iota(jnp.int32, (LANES, LANES), 0)
    c128 = lax.broadcasted_iota(jnp.int32, (LANES, LANES), 1)
    one = phase_ref[up]
    phases = []
    for r in range(2):
        to = r128 + rest[r]
        to = jnp.where(to >= LANES, to - LANES, to)
        turn = (to == c128).astype(jnp.float32).astype(jnp.bfloat16)
        turned = [dot(one[:, p * LANES:(p + 1) * LANES], turn) for p in range(3)]
        turned = jnp.concatenate(turned, axis=1).astype(jnp.bfloat16)
        phases.append(jnp.concatenate([turned] * 3, axis=0))

    def place(start, sent):
        for v in range(paired):
            i = start + v
            src = jnp.where(upper, partner[base + i] - half_total - base, i)
            x = x_ref[jnp.minimum(jnp.maximum(src, 0), views - 1)]
            hi = x.astype(jnp.bfloat16)
            left = x - hi.astype(jnp.float32)
            md = left.astype(jnp.bfloat16)
            lo = (left - md.astype(jnp.float32)).astype(jnp.bfloat16)
            moved = dot(pick, jnp.concatenate([hi, md, lo], axis=1)).astype(jnp.bfloat16)
            for r in range(2):
                mv[r, v * blocks:(v + 1) * blocks, :] = moved[r * blocks:(r + 1) * blocks]
        for r in range(2):
            z[r] = dot(mv[r], phases[r])
        for v in range(paired):
            lines = []
            for r in range(2):
                rows = slice(v * blocks, (v + 1) * blocks)
                y = (
                    z[r, rows, :LANES]
                    + pltpu.roll(z[r, rows, LANES:2 * LANES], 1, 0)
                    + pltpu.roll(z[r, rows, 2 * LANES:], blocks - 1, 0)
                )
                y = -jnp.log(y * (1.0 / 3.0))
                y = jnp.where(lane_b < rest[r], pltpu.roll(y, 1, 0), y)
                lines.append(y)
            st[side, start + v] = weight * jnp.concatenate(lines, axis=0)
            if sent:
                ex_copy(v).start()

    def ex_copy(v):
        i = (1 - up) * paired + v
        return pltpu.make_async_remote_copy(
            src_ref=st.at[side, i], dst_ref=st.at[side, i],
            send_sem=ex_send.at[v], recv_sem=ex_recv.at[v],
            device_id={"views": other}, device_id_type=MESH)

    pl.semaphore_wait(barrier, n + nr - 2)
    place((1 - up) * paired, True)
    place(up * paired, False)

    for k in range(NCOEF):
        acc = None
        for i in range(views):
            term = band[(base + i) * 16 + k] * st[side, i]
            acc = term if acc is None else acc + term
        cbuf[pl.ds(k, vrows, stride=SLOT), :] = acc
    cbuf[pl.ds(NCOEF, vrows, stride=SLOT), :] = jnp.zeros((vrows, LANES), jnp.float32)

    def rs_copy(d):
        to = lax.rem(s + d + 1, half)
        return pltpu.make_async_remote_copy(
            src_ref=cbuf.at[pl.ds(pl.multiple_of(to * strip, 8), strip)], dst_ref=rsbuf.at[d],
            send_sem=rs_send.at[d], recv_sem=rs_recv.at[d],
            device_id={"views": up * half + to}, device_id_type=MESH)

    each(half - 1, lambda d: rs_copy(d).start())
    agbuf[me] = cbuf[pl.ds(pl.multiple_of(s * strip, 8), strip), :]

    def rs_add(d):
        rs_copy(d).wait_recv()
        agbuf[me] = agbuf[me] + rsbuf[d]

    each(half - 1, rs_add)

    def ag_copy(d):
        return pltpu.make_async_remote_copy(
            src_ref=agbuf.at[me], dst_ref=agbuf.at[me],
            send_sem=ag_send.at[d], recv_sem=ag_recv.at[d],
            device_id={"views": lax.rem(me + d + 1, n)}, device_id_type=MESH)

    each(n - 1, lambda d: ag_copy(d).start())
    each(half - 1, lambda d: rs_copy(d).wait_send())

    def ag_arrive(d):
        frm = lax.rem(me + n - d - 1, n)
        pltpu.make_async_remote_copy(
            src_ref=agbuf.at[frm], dst_ref=agbuf.at[frm],
            send_sem=ag_send.at[d], recv_sem=ag_recv.at[d],
            device_id={"views": frm}, device_id_type=MESH).wait_recv()

    each(n - 1, ag_arrive)
    each(n - 1, lambda d: ag_copy(d).wait_send())

    lap = 2 * blocks - TURNS
    strips_side = agbuf.shape[0] // 2
    flat = agbuf
    rows_id = lax.broadcasted_iota(jnp.int32, (2 * blocks, LANES), 0)
    joins = jnp.logical_and(rows_id >= blocks - lap, rows_id < blocks)
    gone = jnp.logical_and(rows_id >= blocks, rows_id < blocks + lap)
    sums = [jnp.zeros((1, LANES), jnp.float32) for _ in range(GBAND)]
    for k in range(NCOEF):
        pieces = {}
        for sd in range(2):
            first_slot = half if sd == 0 else 0
            per = strip // SLOT
            if per >= 8:
                got = [flat[first_slot + q, pl.ds(k, per, stride=SLOT), :] for q in range(half)]
                pieces[sd] = jnp.concatenate(got, axis=0)
            else:
                got = [flat[first_slot + q, pl.ds(k, per), :] for q in range(half)]
                pieces[sd] = jnp.concatenate(got, axis=0)
        for r in range(2):
            line = jnp.concatenate([pieces[0][r * blocks:(r + 1) * blocks],
                                    pieces[1][r * blocks:(r + 1) * blocks]], axis=0)
            ahead = pltpu.roll(line, 2 * blocks - lap, 0)
            line = jnp.where(joins, line + ahead, jnp.where(gone, 0.0, line))
            full[k, r] = line
            g = k if k < GBAND else k - GBAND + 1
            sums[g] = sums[g] + jnp.sum(line * line, axis=0, keepdims=True)
    pwbuf[0] = jnp.concatenate(sums + [jnp.zeros((8 - GBAND, LANES), jnp.float32)], axis=0)

    def pw_copy(d):
        return pltpu.make_async_remote_copy(
            src_ref=pwbuf.at[0], dst_ref=pwbuf.at[d + 1],
            send_sem=pw_send.at[d], recv_sem=pw_recv.at[d],
            device_id={"rows": lax.rem(my_row + d + 1, nr)}, device_id_type=MESH)

    each(nr - 1, lambda d: pw_copy(d).start())
    for v in range(paired):
        ex_copy(v).wait_send()
    for v in range(paired):
        i = up * paired + v
        pltpu.make_async_remote_copy(
            src_ref=st.at[1 - side, i], dst_ref=st.at[1 - side, i],
            send_sem=ex_send.at[v], recv_sem=ex_recv.at[v],
            device_id={"views": other}, device_id_type=MESH).wait_recv()
    each(nr - 1, lambda d: pw_copy(d).wait_recv())
    total = pwbuf[0]
    for d in range(nr - 1):
        total = total + pwbuf[d + 1]
    power = jnp.sum(total, axis=1, keepdims=True) / (rows_total * WIDE) + SHRINK_FLOOR
    for r in range(2):
        for g in range(GBAND):
            re = full[g, r]
            mag = re * re
            if g:
                im = full[GBAND + g - 1, r]
                mag = mag + im * im
            factor = (1.0 - (g / GBAND) ** 2) * mag / (mag + power[g:g + 1])
            full[g, r] = factor * re
            if g:
                full[GBAND + g - 1, r] = factor * im
    each(nr - 1, lambda d: pw_copy(d).wait_send())

    cos, sin = twist_ref[0], twist_ref[1]
    first = first_ref[...]
    for v in range(paired):
        i = up * paired + v
        lines = []
        for r in range(2):
            line = jnp.concatenate([st[0, i, r * blocks:(r + 1) * blocks],
                                    st[1, i, r * blocks:(r + 1) * blocks]], axis=0)
            for k in range(NCOEF):
                line = line - band[(base + i) * 16 + 8 + k] * full[k, r]
            lines.append(line)
        hi, lo = split(jnp.concatenate(lines, axis=1))
        step = dot(first, jnp.concatenate([hi, lo, hi], axis=0))
        for r in range(2):
            re = step[:PAD, r * LANES:(r + 1) * LANES]
            im = step[PAD:, r * LANES:(r + 1) * LANES]
            at = (2 * v + r) * PAD
            mid[at:at + PAD, :LANES] = re * cos + im * sin
            mid[at:at + PAD, LANES:] = im * cos - re * sin

    hi, lo = split(mid[...])
    spec = dot(hi, fwd_ref[0]) + dot(lo, fwd_ref[0]) + dot(hi, fwd_ref[1])
    resp = resp_ref[...]
    resp = jnp.concatenate([resp, resp], axis=1)
    resp = jnp.concatenate([resp] * (2 * paired), axis=0)
    hi, lo = split(spec * resp)
    mid[...] = dot(hi, inv_ref[0]) + dot(lo, inv_ref[0]) + dot(hi, inv_ref[1])

    last = last_ref[...]
    for v in range(paired):
        res, ims = [], []
        for r in range(2):
            at = (2 * v + r) * PAD
            re = mid[at:at + PAD, :LANES]
            im = mid[at:at + PAD, LANES:]
            res.append(re * cos - im * sin)
            ims.append(im * cos + re * sin)
        both = jnp.concatenate([jnp.concatenate(res, axis=1), jnp.concatenate(ims, axis=1)], axis=0)
        hi, lo = split(both)
        y = dot(last, jnp.concatenate([hi, lo, hi], axis=0))
        for r in range(2):
            out_ref[pl.ds(v * 2 * TURNS + r, TURNS, stride=2), :] = y[:TURNS, r * LANES:(r + 1) * LANES]


def on_device(n, nr, projections, partner, geometry):
    views, row_dev, cols = projections.shape
    assert row_dev == 2
    blocks = cols // LANES
    half = n // 2
    vrows = 2 * blocks
    strip = vrows * SLOT // half
    x = projections.reshape(views, row_dev, blocks, LANES).transpose(0, 2, 1, 3).reshape(views, vrows, LANES)
    tables = (phase_table(),) + ramp_tables(blocks, TURNS - blocks)
    band = jnp.asarray(band_tables(views * half))
    smem = pl.BlockSpec(memory_space=pltpu.SMEM)
    vmem = pl.BlockSpec(memory_space=pltpu.VMEM)
    paired = views // 2
    dma = pltpu.SemaphoreType.DMA
    out = pl.pallas_call(
        functools.partial(kernel, n, nr, views, blocks, row_dev * nr),
        out_shape=jax.ShapeDtypeStruct((paired * 2 * TURNS, LANES), jnp.float32),
        in_specs=[smem] * 3 + [vmem] * (1 + len(tables)),
        out_specs=vmem,
        scratch_shapes=[
            pltpu.VMEM((2, views, vrows, LANES), jnp.float32),
            pltpu.VMEM((vrows * SLOT, LANES), jnp.float32),
            pltpu.VMEM((half - 1, strip, LANES), jnp.float32),
            pltpu.VMEM((n, strip, LANES), jnp.float32),
            pltpu.VMEM((NCOEF, 2, 2 * blocks, LANES), jnp.float32),
            pltpu.VMEM((nr, 8, LANES), jnp.float32),
            pltpu.VMEM((paired * 2 * PAD, 2 * LANES), jnp.float32),
            pltpu.VMEM((2, paired * blocks, 3 * LANES), jnp.bfloat16),
            pltpu.VMEM((2, paired * blocks, 3 * LANES), jnp.float32),
            dma((paired,)), dma((paired,)),
            dma((half - 1,)), dma((half - 1,)),
            dma((n - 1,)), dma((n - 1,)),
            dma((nr - 1,)), dma((nr - 1,)),
        ],
        compiler_params=pltpu.CompilerParams(
            collective_id=0, has_side_effects=True, vmem_limit_bytes=32 * 2**20),
        cost_estimate=pl.CostEstimate(flops=10**9, bytes_accessed=2 * 10**6, transcendentals=131072),
    )(partner, geometry, band, x, *[jnp.asarray(t) for t in tables])
    out = out.reshape(paired, TURNS, 2, LANES).transpose(0, 2, 1, 3)
    return out.reshape(paired, 2, WIDE)


def solution(mesh):
    in_specs = (P("views", "rows", None), P(), P())
    out_specs = P("views", "rows", None)
    n, nr = mesh.shape["views"], mesh.shape["rows"]
    return jax.shard_map(
        functools.partial(on_device, n, nr), mesh=mesh, in_specs=in_specs, out_specs=out_specs, check_vma=False
    )
```

profile of v0, /device:TPU:0, one launch (start us, length us, event | category | flops | bytes accessed | tf_op | source)
XLA Modules:
  0.0 34.0 jit_solution(9446584567373324174)
XLA Ops:
  0.0 0.0 copy-start.1
  0.0 0.0 copy-start.2
  0.0 0.7 %copy-done.1 = s32[2,8]{1,0:T(2,128)S(1)} copy-done((s32[2,8]{1,0:T(2,128)S(1)}, s32[2,8]{1,0:T(2,128)}, u32[]{:S(2)}) %copy-start.1) | copy-done | bytes 88
  0.7 0.0 copy-done.2
  0.7 0.0 copy-start
  0.7 1.0 %copy-done = f32[16,2,4096]{2,1,0:T(2,128)S(1)} copy-done((f32[16,2,4096]{2,1,0:T(2,128)S(1)}, f32[16,2,4096]{2,1,0:T(2,128)}, u32[]{:S(2)}) %copy-start) | copy-done | bytes 524312
  1.7 0.0 copy-start.3
  1.7 0.9 %copy-done.3 = bf16[2,256,256]{2,1,0:T(8,128)(2,1)S(1)} copy-done((bf16[2,256,256]{2,1,0:T(8,128)(2,1)S(1)}, bf16[2,256,256]{2,1,0:T(8,128)(2,1)}, u32[]{:S(2)}) %copy-start.3) | copy-done | bytes 262168
  2.7 0.0 copy-start.4
  2.7 0.9 %copy-done.4 = bf16[2,256,256]{2,1,0:T(8,128)(2,1)S(1)} copy-done((bf16[2,256,256]{2,1,0:T(8,128)(2,1)S(1)}, bf16[2,256,256]{2,1,0:T(8,128)(2,1)}, u32[]{:S(2)}) %copy-start.4) | copy-done | bytes 262168
  3.6 0.0 copy-start.5
  3.6 0.9 %copy-done.5 = bf16[2,128,384]{2,1,0:T(8,128)(2,1)S(1)} copy-done((bf16[2,128,384]{2,1,0:T(8,128)(2,1)S(1)}, bf16[2,128,384]{2,1,0:T(8,128)(2,1)}, u32[]{:S(2)}) %copy-start.5) | copy-done | bytes 196632
  4.6 0.0 copy-start.6
  4.6 0.8 %copy-done.6 = bf16[64,192]{1,0:T(8,128)(2,1)S(1)} copy-done((bf16[64,192]{1,0:T(8,128)(2,1)S(1)}, bf16[64,192]{1,0:T(8,128)(2,1)}, u32[]{:S(2)}) %copy-start.6) | copy-done | bytes 24600
  5.3 0.0 copy-start.7
  5.3 0.8 %copy-done.7 = f32[2,32,128]{2,1,0:T(8,128)S(1)} copy-done((f32[2,32,128]{2,1,0:T(8,128)S(1)}, f32[2,32,128]{2,1,0:T(8,128)}, u32[]{:S(2)}) %copy-start.7) | copy-done | bytes 32792
  6.1 0.0 copy-start.8
  6.1 0.8 %copy-done.8 = bf16[64,192]{1,0:T(8,128)(2,1)S(1)} copy-done((bf16[64,192]{1,0:T(8,128)(2,1)S(1)}, bf16[64,192]{1,0:T(8,128)(2,1)}, u32[]{:S(2)}) %copy-start.8) | copy-done | bytes 24600
  6.8 0.7 %copy-done.9 = f32[32,128]{1,0:T(8,128)S(1)} copy-done((f32[32,128]{1,0:T(8,128)S(1)}, f32[32,128]{1,0:T(8,128)}, u32[]{:S(2)}) %copy-start.9) | copy-done | bytes 16408
  7.5 0.7 %copy-done.10 = f32[1024]{0:T(1024)S(1)} copy-done((f32[1024]{0:T(1024)S(1)}, f32[1024]{0:T(1024)}, u32[]{:S(2)}) %copy-start.10) | copy-done | bytes 4120
  8.2 24.4 %shard_map.109 = f32[960,128]{1,0:T(8,128)S(1)} custom-call(s32[64]{0:T(128)S(1)} %copy-done.2, s32[2,8]{1,0:T(2,128)S(1)} %copy-done.1, f32[1024]{0:T(1024)S(1)} %copy-done.10, f32[16,64,128]{2,1,0:T(8,128)S(1)} %bitcast.12, bf16[2,128,384]{2,1,0:T(8,128)(2,1)S(1)} %copy-done.5, bf16[64,192]{1,0:T(8,128)(2,1)S(1)} %copy-done.8, ...), custom_call_target="tpu_custom_call" | custom-call | flops 1000000000 | bytes 2000000 | tf_op jit(solution)/shard_map/pallas_call | solution.py:369
  32.7 0.1 copy.18
  32.7 0.1 reshape.15
  32.8 1.2 %copy.16 = f32[8,2,7680]{2,1,0:T(2,128)} copy(f32[8,2,7680]{2,0,1:T(8,128)S(1)} %reshape.15) | data formatting | bytes 983040 | tf_op jit(solution)/shard_map/reshape | solution.py:394
  (2 shorter events, 0.0 us)
Async XLA Ops:
  0.0 0.7 %copy-start.1 = (s32[2,8]{1,0:T(2,128)S(1)}, s32[2,8]{1,0:T(2,128)}, u32[]{:S(2)}) copy-start(s32[2,8]{1,0:T(2,128)} %geometry.1) | copy-start | bytes 196
  0.0 0.7 %copy-start.2 = (s32[64]{0:T(128)S(1)}, s32[64]{0:T(128)}, u32[]{:S(2)}) copy-start(s32[64]{0:T(128)} %partner.1) | copy-start | bytes 772
  0.7 1.0 %copy-start = (f32[16,2,4096]{2,1,0:T(2,128)S(1)}, f32[16,2,4096]{2,1,0:T(2,128)}, u32[]{:S(2)}) copy-start(f32[16,2,4096]{2,1,0:T(2,128)} %param.11) | copy-start | bytes 1572868
  1.7 0.9 %copy-start.3 = (bf16[2,256,256]{2,1,0:T(8,128)(2,1)S(1)}, bf16[2,256,256]{2,1,0:T(8,128)(2,1)}, u32[]{:S(2)}) copy-start(bf16[2,256,256]{2,1,0:T(8,128)(2,1)} %constant.20.clone.inv_ref) | copy-start | bytes 786436
  2.7 0.9 %copy-start.4 = (bf16[2,256,256]{2,1,0:T(8,128)(2,1)S(1)}, bf16[2,256,256]{2,1,0:T(8,128)(2,1)}, u32[]{:S(2)}) copy-start(bf16[2,256,256]{2,1,0:T(8,128)(2,1)} %constant.19.clone.fwd_ref) | copy-start | bytes 786436
  3.6 0.9 %copy-start.5 = (bf16[2,128,384]{2,1,0:T(8,128)(2,1)S(1)}, bf16[2,128,384]{2,1,0:T(8,128)(2,1)}, u32[]{:S(2)}) copy-start(bf16[2,128,384]{2,1,0:T(8,128)(2,1)} %constant.17.clone.phase_ref) | copy-start | bytes 589828
  4.6 0.8 %copy-start.6 = (bf16[64,192]{1,0:T(8,128)(2,1)S(1)}, bf16[64,192]{1,0:T(8,128)(2,1)}, u32[]{:S(2)}) copy-start(bf16[64,192]{1,0:T(8,128)(2,1)} %constant.23.clone.last_ref) | copy-start | bytes 73732
  5.3 0.8 %copy-start.7 = (f32[2,32,128]{2,1,0:T(8,128)S(1)}, f32[2,32,128]{2,1,0:T(8,128)}, u32[]{:S(2)}) copy-start(f32[2,32,128]{2,1,0:T(8,128)} %constant.21.clone.twist_ref) | copy-start | bytes 98308
  6.1 0.8 %copy-start.8 = (bf16[64,192]{1,0:T(8,128)(2,1)S(1)}, bf16[64,192]{1,0:T(8,128)(2,1)}, u32[]{:S(2)}) copy-start(bf16[64,192]{1,0:T(8,128)(2,1)} %constant.18.clone.first_ref) | copy-start | bytes 73732
  6.8 0.7 %copy-start.9 = (f32[32,128]{1,0:T(8,128)S(1)}, f32[32,128]{1,0:T(8,128)}, u32[]{:S(2)}) copy-start(f32[32,128]{1,0:T(8,128)} %constant.22.clone.resp_ref) | copy-start | bytes 49156
  7.5 0.7 %copy-start.10 = (f32[1024]{0:T(1024)S(1)}, f32[1024]{0:T(1024)}, u32[]{:S(2)}) copy-start(f32[1024]{0:T(1024)} %constant.16.clone.band) | copy-start | bytes 12292
where the time goes:
time: 34.5 us; the launch traced here: 34 us
  Pallas kernels  24.4 us (71%)
  local copies, waits for them, and re-layouts  9.52 us (28%)
    pallas_call x1, Pallas kernels, on_device(): pl.pallas_call(functools.partial(kernel, n, nr, views, blocks, row_dev *...  24.4 us
    unnamed x22, local copies, waits for them, and re-layouts  8.22 us
    reshape x2, local copies, waits for them, and re-layouts, on_device(): return out.reshape(paired, 2, WIDE)  1.25 us

commit v1 on v0

--- a/solution.py
+++ b/solution.py
@@ -75,7 +75,7 @@
     last = np.concatenate([np.cos(ang), -np.sin(ang)], axis=1) * np.concatenate([live, live])[:, 0]
     lhi, llo = split_np(last)
     last = np.concatenate([lhi, lhi, llo], axis=1)
-    return first, np.stack(fwd), np.stack(inv), twist, response.astype(np.float32), last
+    return first, twist, np.stack(fwd), response.astype(np.float32), np.stack(inv), last
 
 
 def band_tables(half_total):
@@ -95,10 +95,11 @@
 
 def kernel(
     n, nr, views, blocks, rows_total,
-    partner, geometry, band, x_ref, phase_ref, first_ref, fwd_ref, inv_ref, twist_ref, resp_ref, last_ref,
+    partner_hbm, geometry_hbm, band_hbm, x_hbm, phase_hbm, first_hbm, twist_hbm, fwd_hbm, resp_hbm, inv_hbm, last_hbm,
     out_ref,
+    partner, geometry, band, x_ref, phase_ref, first_ref, twist_ref, fwd_ref, resp_ref, inv_ref, last_ref, ld_sem,
     st, cbuf, rsbuf, agbuf, full, pwbuf, mid, mv, z,
-    ex_send, ex_recv, rs_send, rs_recv, ag_send, ag_recv, pw_send, pw_recv,
+    ex_send, ex_recv, rs_send, rs_recv, ag_send, ag_recv, fw_send, fw_recv, pw_send, pw_recv,
 ):
     half = n // 2
     paired = views // 2
@@ -123,6 +124,15 @@
 
     each(n - 1, greet_view)
     each(nr - 1, greet_row)
+
+    sources = (geometry_hbm, partner_hbm, x_hbm, phase_hbm, band_hbm, first_hbm, twist_hbm, fwd_hbm, resp_hbm, inv_hbm,
+               last_hbm)
+    targets = (geometry, partner, x_ref, phase_ref, band, first_ref, twist_ref, fwd_ref, resp_ref, inv_ref, last_ref)
+    loads = [pltpu.make_async_copy(a, b, ld_sem.at[i]) for i, (a, b) in enumerate(zip(sources, targets))]
+    for load in loads:
+        load.start()
+    for load in loads[:4]:
+        load.wait()
 
     margins = [geometry[0, my_row * 2 + r] for r in range(2)]
     offsets = [geometry[1, my_row * 2 + r] for r in range(2)]
@@ -204,6 +214,8 @@
     place((1 - up) * paired, True)
     place(up * paired, False)
 
+    for load in loads[4:]:
+        load.wait()
     for k in range(NCOEF):
         acc = None
         for i in range(views):
@@ -228,24 +240,41 @@
 
     each(half - 1, rs_add)
 
-    def ag_copy(d):
+    par = lax.rem(me, 2)
+    sibling = me + 1 - 2 * par
+
+    def ag_copy(d, slot):
         return pltpu.make_async_remote_copy(
-            src_ref=agbuf.at[me], dst_ref=agbuf.at[me],
+            src_ref=agbuf.at[slot], dst_ref=agbuf.at[slot],
             send_sem=ag_send.at[d], recv_sem=ag_recv.at[d],
-            device_id={"views": lax.rem(me + d + 1, n)}, device_id_type=MESH)
-
-    each(n - 1, lambda d: ag_copy(d).start())
+            device_id={"views": lax.rem(me + 2 * d + 2, n)}, device_id_type=MESH)
+
+    def fw_copy(d, slot):
+        return pltpu.make_async_remote_copy(
+            src_ref=agbuf.at[slot], dst_ref=agbuf.at[slot],
+            send_sem=fw_send.at[d], recv_sem=fw_recv.at[d],
+            device_id={"views": sibling}, device_id_type=MESH)
+
+    def came(d):
+        return lax.rem(me + n - 2 * d - 2, n)
+
+    def came_sibling(d):
+        return lax.rem(sibling + n - 2 * d - 2, n)
+
+    each(half - 1, lambda d: ag_copy(d, me).start())
+    fw_copy(half - 1, me).start()
     each(half - 1, lambda d: rs_copy(d).wait_send())
 
-    def ag_arrive(d):
-        frm = lax.rem(me + n - d - 1, n)
-        pltpu.make_async_remote_copy(
-            src_ref=agbuf.at[frm], dst_ref=agbuf.at[frm],
-            send_sem=ag_send.at[d], recv_sem=ag_recv.at[d],
-            device_id={"views": frm}, device_id_type=MESH).wait_recv()
-
-    each(n - 1, ag_arrive)
-    each(n - 1, lambda d: ag_copy(d).wait_send())
+    def forward(d):
+        ag_copy(d, came(d)).wait_recv()
+        fw_copy(d, came(d)).start()
+
+    each(half - 1, forward)
+    fw_copy(half - 1, sibling).wait_recv()
+    each(half - 1, lambda d: fw_copy(d, came_sibling(d)).wait_recv())
+    each(half - 1, lambda d: ag_copy(d, me).wait_send())
+    each(half - 1, lambda d: fw_copy(d, came(d)).wait_send())
+    fw_copy(half - 1, me).wait_send()
 
     lap = 2 * blocks - TURNS
     strips_side = agbuf.shape[0] // 2
@@ -362,16 +391,21 @@
     x = projections.reshape(views, row_dev, blocks, LANES).transpose(0, 2, 1, 3).reshape(views, vrows, LANES)
     tables = (phase_table(),) + ramp_tables(blocks, TURNS - blocks)
     band = jnp.asarray(band_tables(views * half))
-    smem = pl.BlockSpec(memory_space=pltpu.SMEM)
     vmem = pl.BlockSpec(memory_space=pltpu.VMEM)
     paired = views // 2
     dma = pltpu.SemaphoreType.DMA
     out = pl.pallas_call(
         functools.partial(kernel, n, nr, views, blocks, row_dev * nr),
         out_shape=jax.ShapeDtypeStruct((paired * 2 * TURNS, LANES), jnp.float32),
-        in_specs=[smem] * 3 + [vmem] * (1 + len(tables)),
+        in_specs=[pl.BlockSpec(memory_space=pl.ANY)] * (4 + len(tables)),
         out_specs=vmem,
         scratch_shapes=[
+            pltpu.SMEM(partner.shape, jnp.int32),
+            pltpu.SMEM(geometry.shape, jnp.int32),
+            pltpu.SMEM(band.shape, jnp.float32),
+            pltpu.VMEM(x.shape, jnp.float32),
+            *[pltpu.VMEM(t.shape, t.dtype) for t in tables],
+            dma((4 + len(tables),)),
             pltpu.VMEM((2, views, vrows, LANES), jnp.float32),
             pltpu.VMEM((vrows * SLOT, LANES), jnp.float32),
             pltpu.VMEM((half - 1, strip, LANES), jnp.float32),
@@ -383,11 +417,12 @@
             pltpu.VMEM((2, paired * blocks, 3 * LANES), jnp.float32),
             dma((paired,)), dma((paired,)),
             dma((half - 1,)), dma((half - 1,)),
-            dma((n - 1,)), dma((n - 1,)),
+            dma((half - 1,)), dma((half - 1,)),
+            dma((half,)), dma((half,)),
             dma((nr - 1,)), dma((nr - 1,)),
         ],
         compiler_params=pltpu.CompilerParams(
-            collective_id=0, has_side_effects=True, vmem_limit_bytes=32 * 2**20),
+            collective_id=0, has_side_effects=True, vmem_limit_bytes=56 * 2**20),
         cost_estimate=pl.CostEstimate(flops=10**9, bytes_accessed=2 * 10**6, transcendentals=131072),
     )(partner, geometry, band, x, *[jnp.asarray(t) for t in tables])
     out = out.reshape(paired, TURNS, 2, LANES).transpose(0, 2, 1, 3)

time: 34.5 us -> 26 us (0.75); the launches traced: 34 us -> 25.9 us
  local copies, waits for them, and re-layouts: 9.52 us -> 2.33 us
  Pallas kernels: 24.4 us -> 23.5 us
    unnamed x22 -> x0, local copies, waits for them, and re-layouts: 8.22 us -> none
    reshape x1, local copies, waits for them, and re-layouts: 0.05 us -> 1.09 us  [on_device(): out = out.reshape(paired, TURNS, 2, LANES).transpose(0, 2, 1, 3)]
    pallas_call x1, Pallas kernels: 24.4 us -> 23.5 us  [on_device(): pl.pallas_call(functools.partial(kernel, n, nr, views, blocks, row_dev *...]
where the time goes in v1:
time: 26 us; the launch traced here: 25.9 us
  Pallas kernels  23.5 us (90%)
  local copies, waits for them, and re-layouts  2.33 us (9%)
    pallas_call x1, Pallas kernels, on_device(): pl.pallas_call(functools.partial(kernel, n, nr, views, blocks, row_dev *...  23.5 us
    reshape x2, local copies, waits for them, and re-layouts, on_device(): return out.reshape(paired, 2, WIDE)  1.25 us
    reshape x1, local copies, waits for them, and re-layouts, on_device(): out = out.reshape(paired, TURNS, 2, LANES).transpose(0, 2, 1, 3)  1.09 us

profile of v1, /device:TPU:0, one launch (start us, length us, event | category | flops | bytes accessed | tf_op | source)
XLA Modules:
  0.0 25.9 jit_solution(14769211349290778477)
XLA Ops:
  0.0 23.5 %shard_map.109 = f32[960,128]{1,0:T(8,128)} custom-call(s32[64]{0:T(128)} %partner_hbm.1, s32[2,8]{1,0:T(2,128)} %geometry_hbm.1, f32[1024]{0:T(1024)} %constant.16.clone.band_hbm, f32[16,64,128]{2,1,0:T(8,128)} %bitcast.13, bf16[2,128,384]{2,1,0:T(8,128)(2,1)} %constant.17.clone.phase_hbm, bf16[64,192]{1,0:T(8,128)(2,1)} %constant.18.clone.first_hbm, ...), custom_call_target="tpu_custom_call" | custom-call | flops 1000000000 | bytes 2000000 | tf_op jit(solution)/shard_map/pallas_call | solution.py:397
  23.5 1.1 %copy.18 = f32[8,60,2,128]{3,1,0,2:T(8,128)S(1)} copy(f32[8,60,2,128]{3,2,1,0:T(2,128)} %bitcast.12) | data formatting | bytes 983040 | tf_op jit(solution)/shard_map/reshape | solution.py:428
  24.6 0.1 reshape.15
  24.7 1.2 %copy.16 = f32[8,2,7680]{2,1,0:T(2,128)} copy(f32[8,2,7680]{2,0,1:T(8,128)S(1)} %reshape.15) | data formatting | bytes 983040 | tf_op jit(solution)/shard_map/reshape | solution.py:429

commit v2 on v1

--- a/solution.py
+++ b/solution.py
@@ -98,8 +98,9 @@
     partner_hbm, geometry_hbm, band_hbm, x_hbm, phase_hbm, first_hbm, twist_hbm, fwd_hbm, resp_hbm, inv_hbm, last_hbm,
     out_ref,
     partner, geometry, band, x_ref, phase_ref, first_ref, twist_ref, fwd_ref, resp_ref, inv_ref, last_ref, ld_sem,
-    st, cbuf, rsbuf, agbuf, full, pwbuf, mid, mv, z,
-    ex_send, ex_recv, rs_send, rs_recv, ag_send, ag_recv, fw_send, fw_recv, pw_send, pw_recv,
+    st, cbuf, rsbuf, agbuf, full, pwbuf, pvbuf, lapbuf, mid, mv, z,
+    ex_send, ex_recv, rs_send, rs_recv, ag_send, ag_recv, fw_send, fw_recv, pw_send, pw_recv, pv_send, pv_recv,
+    lap_send, lap_recv,
 ):
     half = n // 2
     paired = views // 2
@@ -173,7 +174,7 @@
         turned = jnp.concatenate(turned, axis=1).astype(jnp.bfloat16)
         phases.append(jnp.concatenate([turned] * 3, axis=0))
 
-    def place(start, sent):
+    def place(start):
         for v in range(paired):
             i = start + v
             src = jnp.where(upper, partner[base + i] - half_total - base, i)
@@ -200,8 +201,6 @@
                 y = jnp.where(lane_b < rest[r], pltpu.roll(y, 1, 0), y)
                 lines.append(y)
             st[side, start + v] = weight * jnp.concatenate(lines, axis=0)
-            if sent:
-                ex_copy(v).start()
 
     def ex_copy(v):
         i = (1 - up) * paired + v
@@ -210,9 +209,8 @@
             send_sem=ex_send.at[v], recv_sem=ex_recv.at[v],
             device_id={"views": other}, device_id_type=MESH)
 
-    pl.semaphore_wait(barrier, n + nr - 2)
-    place((1 - up) * paired, True)
-    place(up * paired, False)
+    place(0)
+    place(paired)
 
     for load in loads[4:]:
         load.wait()
@@ -224,6 +222,8 @@
         cbuf[pl.ds(k, vrows, stride=SLOT), :] = acc
     cbuf[pl.ds(NCOEF, vrows, stride=SLOT), :] = jnp.zeros((vrows, LANES), jnp.float32)
 
+    pl.semaphore_wait(barrier, n + nr - 2)
+
     def rs_copy(d):
         to = lax.rem(s + d + 1, half)
         return pltpu.make_async_remote_copy(
@@ -231,7 +231,28 @@
             send_sem=rs_send.at[d], recv_sem=rs_recv.at[d],
             device_id={"views": up * half + to}, device_id_type=MESH)
 
+    lap = 2 * blocks - TURNS
+    per = strip // SLOT
+    piece = min(per, lap)
+    pieces = [(r * blocks + q * piece, r * blocks + blocks - lap + q * piece)
+              for r in range(2) for q in range(lap // piece)]
+
+    def lap_copy(m, e):
+        low, high = pieces[m]
+        return pltpu.make_async_remote_copy(
+            src_ref=cbuf.at[pl.ds(low * SLOT, piece * SLOT)], dst_ref=lapbuf.at[e],
+            send_sem=lap_send.at[m], recv_sem=lap_recv.at[e],
+            device_id={"views": half + high // per}, device_id_type=MESH)
+
     each(half - 1, lambda d: rs_copy(d).start())
+
+    @pl.when(jnp.logical_not(upper))
+    def _():
+        for m in range(len(pieces)):
+            lap_copy(m, me).start()
+
+    for v in range(paired):
+        ex_copy(v).start()
     agbuf[me] = cbuf[pl.ds(pl.multiple_of(s * strip, 8), strip), :]
 
     def rs_add(d):
@@ -239,6 +260,20 @@
         agbuf[me] = agbuf[me] + rsbuf[d]
 
     each(half - 1, rs_add)
+    for m, (low, high) in enumerate(pieces):
+        @pl.when(jnp.logical_and(upper, s == high // per))
+        def _():
+            at = pl.ds(high % per * SLOT, piece * SLOT)
+
+            def lap_add(e):
+                lap_copy(m, e).wait_recv()
+                agbuf[me, at, :] = agbuf[me, at, :] + lapbuf[e]
+
+            each(half, lap_add)
+
+        @pl.when(jnp.logical_and(jnp.logical_not(upper), s == low // per))
+        def _():
+            agbuf[me, pl.ds(low % per * SLOT, piece * SLOT), :] = jnp.zeros((piece * SLOT, LANES), jnp.float32)
 
     par = lax.rem(me, 2)
     sibling = me + 1 - 2 * par
@@ -261,56 +296,58 @@
     def came_sibling(d):
         return lax.rem(sibling + n - 2 * d - 2, n)
 
+    def pw_copy(d):
+        return pltpu.make_async_remote_copy(
+            src_ref=pwbuf.at[0], dst_ref=pwbuf.at[d + 1],
+            send_sem=pw_send.at[d], recv_sem=pw_recv.at[d],
+            device_id={"rows": lax.rem(my_row + d + 1, nr)}, device_id_type=MESH)
+
+    def pv_copy(d):
+        return pltpu.make_async_remote_copy(
+            src_ref=pvbuf.at[0], dst_ref=pvbuf.at[d + 1],
+            send_sem=pv_send.at[d], recv_sem=pv_recv.at[d],
+            device_id={"views": lax.rem(me + d + 1, n)}, device_id_type=MESH)
+
     each(half - 1, lambda d: ag_copy(d, me).start())
     fw_copy(half - 1, me).start()
+    mine = agbuf[me]
+    mine = mine * mine
+    acc = mine[:SLOT]
+    for q in range(1, per):
+        acc = acc + mine[q * SLOT:(q + 1) * SLOT]
+    pwbuf[0] = acc
+    each(nr - 1, lambda d: pw_copy(d).start())
     each(half - 1, lambda d: rs_copy(d).wait_send())
+
+    @pl.when(jnp.logical_not(upper))
+    def _():
+        for m in range(len(pieces)):
+            lap_copy(m, me).wait_send()
 
     def forward(d):
         ag_copy(d, came(d)).wait_recv()
         fw_copy(d, came(d)).start()
 
     each(half - 1, forward)
+    each(nr - 1, lambda d: pw_copy(d).wait_recv())
+    acc = pwbuf[0]
+    for d in range(nr - 1):
+        acc = acc + pwbuf[d + 1]
+    pvbuf[0] = acc
+    each(n - 1, lambda d: pv_copy(d).start())
     fw_copy(half - 1, sibling).wait_recv()
     each(half - 1, lambda d: fw_copy(d, came_sibling(d)).wait_recv())
     each(half - 1, lambda d: ag_copy(d, me).wait_send())
     each(half - 1, lambda d: fw_copy(d, came(d)).wait_send())
     fw_copy(half - 1, me).wait_send()
 
-    lap = 2 * blocks - TURNS
-    strips_side = agbuf.shape[0] // 2
-    flat = agbuf
-    rows_id = lax.broadcasted_iota(jnp.int32, (2 * blocks, LANES), 0)
-    joins = jnp.logical_and(rows_id >= blocks - lap, rows_id < blocks)
-    gone = jnp.logical_and(rows_id >= blocks, rows_id < blocks + lap)
-    sums = [jnp.zeros((1, LANES), jnp.float32) for _ in range(GBAND)]
     for k in range(NCOEF):
-        pieces = {}
-        for sd in range(2):
-            first_slot = half if sd == 0 else 0
-            per = strip // SLOT
-            if per >= 8:
-                got = [flat[first_slot + q, pl.ds(k, per, stride=SLOT), :] for q in range(half)]
-                pieces[sd] = jnp.concatenate(got, axis=0)
-            else:
-                got = [flat[first_slot + q, pl.ds(k, per), :] for q in range(half)]
-                pieces[sd] = jnp.concatenate(got, axis=0)
-        for r in range(2):
-            line = jnp.concatenate([pieces[0][r * blocks:(r + 1) * blocks],
-                                    pieces[1][r * blocks:(r + 1) * blocks]], axis=0)
-            ahead = pltpu.roll(line, 2 * blocks - lap, 0)
-            line = jnp.where(joins, line + ahead, jnp.where(gone, 0.0, line))
-            full[k, r] = line
-            g = k if k < GBAND else k - GBAND + 1
-            sums[g] = sums[g] + jnp.sum(line * line, axis=0, keepdims=True)
-    pwbuf[0] = jnp.concatenate(sums + [jnp.zeros((8 - GBAND, LANES), jnp.float32)], axis=0)
-
-    def pw_copy(d):
-        return pltpu.make_async_remote_copy(
-            src_ref=pwbuf.at[0], dst_ref=pwbuf.at[d + 1],
-            send_sem=pw_send.at[d], recv_sem=pw_recv.at[d],
-            device_id={"rows": lax.rem(my_row + d + 1, nr)}, device_id_type=MESH)
-
-    each(nr - 1, lambda d: pw_copy(d).start())
+        sides = []
+        for first_slot in (half, 0):
+            got = [agbuf[first_slot + q, pl.ds(k, per, stride=SLOT), :] for q in range(half)]
+            sides.append(jnp.concatenate(got, axis=0))
+        for r in range(2):
+            full[k, r] = jnp.concatenate([side_k[r * blocks:(r + 1) * blocks] for side_k in sides], axis=0)
     for v in range(paired):
         ex_copy(v).wait_send()
     for v in range(paired):
@@ -319,11 +356,16 @@
             src_ref=st.at[1 - side, i], dst_ref=st.at[1 - side, i],
             send_sem=ex_send.at[v], recv_sem=ex_recv.at[v],
             device_id={"views": other}, device_id_type=MESH).wait_recv()
-    each(nr - 1, lambda d: pw_copy(d).wait_recv())
-    total = pwbuf[0]
-    for d in range(nr - 1):
-        total = total + pwbuf[d + 1]
-    power = jnp.sum(total, axis=1, keepdims=True) / (rows_total * WIDE) + SHRINK_FLOOR
+    each(n - 1, lambda d: pv_copy(d).wait_recv())
+    total = pvbuf[0]
+    if n <= 16:
+        for d in range(n - 1):
+            total = total + pvbuf[d + 1]
+    else:
+        total = lax.fori_loop(1, n, lambda d, c: c + pvbuf[d], total)
+    total = jnp.sum(total, axis=1, keepdims=True)
+    power = [total[g:g + 1] + (total[GBAND + g - 1:GBAND + g] if g else 0.0) for g in range(GBAND)]
+    power = [p / (rows_total * WIDE) + SHRINK_FLOOR for p in power]
     for r in range(2):
         for g in range(GBAND):
             re = full[g, r]
@@ -331,11 +373,12 @@
             if g:
                 im = full[GBAND + g - 1, r]
                 mag = mag + im * im
-            factor = (1.0 - (g / GBAND) ** 2) * mag / (mag + power[g:g + 1])
+            factor = (1.0 - (g / GBAND) ** 2) * mag / (mag + power[g])
             full[g, r] = factor * re
             if g:
                 full[GBAND + g - 1, r] = factor * im
     each(nr - 1, lambda d: pw_copy(d).wait_send())
+    each(n - 1, lambda d: pv_copy(d).wait_send())
 
     cos, sin = twist_ref[0], twist_ref[1]
     first = first_ref[...]
@@ -388,6 +431,8 @@
     half = n // 2
     vrows = 2 * blocks
     strip = vrows * SLOT // half
+    lap = 2 * blocks - TURNS
+    piece = min(strip // SLOT, lap)
     x = projections.reshape(views, row_dev, blocks, LANES).transpose(0, 2, 1, 3).reshape(views, vrows, LANES)
     tables = (phase_table(),) + ramp_tables(blocks, TURNS - blocks)
     band = jnp.asarray(band_tables(views * half))
@@ -411,7 +456,9 @@
             pltpu.VMEM((half - 1, strip, LANES), jnp.float32),
             pltpu.VMEM((n, strip, LANES), jnp.float32),
             pltpu.VMEM((NCOEF, 2, 2 * blocks, LANES), jnp.float32),
-            pltpu.VMEM((nr, 8, LANES), jnp.float32),
+            pltpu.VMEM((nr, SLOT, LANES), jnp.float32),
+            pltpu.VMEM((n, SLOT, LANES), jnp.float32),
+            pltpu.VMEM((half, piece * SLOT, LANES), jnp.float32),
             pltpu.VMEM((paired * 2 * PAD, 2 * LANES), jnp.float32),
             pltpu.VMEM((2, paired * blocks, 3 * LANES), jnp.bfloat16),
             pltpu.VMEM((2, paired * blocks, 3 * LANES), jnp.float32),
@@ -420,6 +467,8 @@
             dma((half - 1,)), dma((half - 1,)),
             dma((half,)), dma((half,)),
             dma((nr - 1,)), dma((nr - 1,)),
+            dma((n - 1,)), dma((n - 1,)),
+            dma((2 * (lap // piece),)), dma((half,)),
         ],
         compiler_params=pltpu.CompilerParams(
             collective_id=0, has_side_effects=True, vmem_limit_bytes=56 * 2**20),

time: 26 us -> 24.7 us (0.950)
  Pallas kernels: 23.5 us -> 22.2 us
    pallas_call x1, Pallas kernels: 23.5 us -> 22.2 us  [on_device(): pl.pallas_call(functools.partial(kernel, n, nr, views, blocks, row_dev *...]
where the time goes in v2:
time: 24.7 us; the launch traced here: 24.5 us
  Pallas kernels  22.2 us (90%)
  local copies, waits for them, and re-layouts  2.33 us (9%)
    pallas_call x1, Pallas kernels, on_device(): pl.pallas_call(functools.partial(kernel, n, nr, views, blocks, row_dev *...  22.2 us
    reshape x2, local copies, waits for them, and re-layouts, on_device(): return out.reshape(paired, 2, WIDE)  1.25 us
    reshape x1, local copies, waits for them, and re-layouts, on_device(): out = out.reshape(paired, TURNS, 2, LANES).transpose(0, 2, 1, 3)  1.09 us

profile of v2, /device:TPU:0, one launch (start us, length us, event | category | flops | bytes accessed | tf_op | source)
XLA Modules:
  0.0 24.5 jit_solution(5488673729524338063)
XLA Ops:
  0.0 22.2 %shard_map.109 = f32[960,128]{1,0:T(8,128)} custom-call(s32[64]{0:T(128)} %partner_hbm.1, s32[2,8]{1,0:T(2,128)} %geometry_hbm.1, f32[1024]{0:T(1024)} %constant.16.clone.band_hbm, f32[16,64,128]{2,1,0:T(8,128)} %bitcast.13, bf16[2,128,384]{2,1,0:T(8,128)(2,1)} %constant.17.clone.phase_hbm, bf16[64,192]{1,0:T(8,128)(2,1)} %constant.18.clone.first_hbm, ...), custom_call_target="tpu_custom_call" | custom-call | flops 1000000000 | bytes 2000000 | tf_op jit(solution)/shard_map/pallas_call | solution.py:442
  22.2 1.1 %copy.18 = f32[8,60,2,128]{3,1,0,2:T(8,128)S(1)} copy(f32[8,60,2,128]{3,2,1,0:T(2,128)} %bitcast.12) | data formatting | bytes 983040 | tf_op jit(solution)/shard_map/reshape | solution.py:477
  23.3 0.1 reshape.15
  23.4 1.2 %copy.16 = f32[8,2,7680]{2,1,0:T(2,128)} copy(f32[8,2,7680]{2,0,1:T(8,128)S(1)} %reshape.15) | data formatting | bytes 983040 | tf_op jit(solution)/shard_map/reshape | solution.py:478

commit v3 on v2

--- a/solution.py
+++ b/solution.py
@@ -22,7 +22,7 @@
 
 
 def each(count, body):
-    if count <= 16:
+    if count <= 32:
         for i in range(count):
             body(i)
     else:
@@ -98,8 +98,8 @@
     partner_hbm, geometry_hbm, band_hbm, x_hbm, phase_hbm, first_hbm, twist_hbm, fwd_hbm, resp_hbm, inv_hbm, last_hbm,
     out_ref,
     partner, geometry, band, x_ref, phase_ref, first_ref, twist_ref, fwd_ref, resp_ref, inv_ref, last_ref, ld_sem,
-    st, cbuf, rsbuf, agbuf, full, pwbuf, pvbuf, lapbuf, mid, mv, z,
-    ex_send, ex_recv, rs_send, rs_recv, ag_send, ag_recv, fw_send, fw_recv, pw_send, pw_recv, pv_send, pv_recv,
+    st, cbuf, rsbuf, agbuf, full, pvbuf, lapbuf, mid, mv, z,
+    ex_send, ex_recv, rs_send, rs_recv, ag_send, ag_recv, fw_send, fw_recv, pv_send, pv_recv,
     lap_send, lap_recv,
 ):
     half = n // 2
@@ -117,14 +117,11 @@
 
     barrier = pltpu.get_barrier_semaphore()
 
-    def greet_view(d):
-        pl.semaphore_signal(barrier, inc=1, device_id={"views": lax.rem(me + d + 1, n)}, device_id_type=MESH)
-
-    def greet_row(d):
-        pl.semaphore_signal(barrier, inc=1, device_id={"rows": lax.rem(my_row + d + 1, nr)}, device_id_type=MESH)
-
-    each(n - 1, greet_view)
-    each(nr - 1, greet_row)
+    def greet(d):
+        to = lax.rem(my_row * n + me + d + 1, n * nr)
+        pl.semaphore_signal(barrier, inc=1, device_id={"views": lax.rem(to, n), "rows": to // n}, device_id_type=MESH)
+
+    each(n * nr - 1, greet)
 
     sources = (geometry_hbm, partner_hbm, x_hbm, phase_hbm, band_hbm, first_hbm, twist_hbm, fwd_hbm, resp_hbm, inv_hbm,
                last_hbm)
@@ -222,7 +219,7 @@
         cbuf[pl.ds(k, vrows, stride=SLOT), :] = acc
     cbuf[pl.ds(NCOEF, vrows, stride=SLOT), :] = jnp.zeros((vrows, LANES), jnp.float32)
 
-    pl.semaphore_wait(barrier, n + nr - 2)
+    pl.semaphore_wait(barrier, n * nr - 1)
 
     def rs_copy(d):
         to = lax.rem(s + d + 1, half)
@@ -296,17 +293,15 @@
     def came_sibling(d):
         return lax.rem(sibling + n - 2 * d - 2, n)
 
-    def pw_copy(d):
-        return pltpu.make_async_remote_copy(
-            src_ref=pwbuf.at[0], dst_ref=pwbuf.at[d + 1],
-            send_sem=pw_send.at[d], recv_sem=pw_recv.at[d],
-            device_id={"rows": lax.rem(my_row + d + 1, nr)}, device_id_type=MESH)
+    everyone = n * nr
+    place_id = my_row * n + me
 
     def pv_copy(d):
+        to = lax.rem(place_id + d + 1, everyone)
         return pltpu.make_async_remote_copy(
             src_ref=pvbuf.at[0], dst_ref=pvbuf.at[d + 1],
             send_sem=pv_send.at[d], recv_sem=pv_recv.at[d],
-            device_id={"views": lax.rem(me + d + 1, n)}, device_id_type=MESH)
+            device_id={"views": lax.rem(to, n), "rows": to // n}, device_id_type=MESH)
 
     each(half - 1, lambda d: ag_copy(d, me).start())
     fw_copy(half - 1, me).start()
@@ -315,8 +310,8 @@
     acc = mine[:SLOT]
     for q in range(1, per):
         acc = acc + mine[q * SLOT:(q + 1) * SLOT]
-    pwbuf[0] = acc
-    each(nr - 1, lambda d: pw_copy(d).start())
+    pvbuf[0] = acc
+    each(everyone - 1, lambda d: pv_copy(d).start())
     each(half - 1, lambda d: rs_copy(d).wait_send())
 
     @pl.when(jnp.logical_not(upper))
@@ -329,12 +324,6 @@
         fw_copy(d, came(d)).start()
 
     each(half - 1, forward)
-    each(nr - 1, lambda d: pw_copy(d).wait_recv())
-    acc = pwbuf[0]
-    for d in range(nr - 1):
-        acc = acc + pwbuf[d + 1]
-    pvbuf[0] = acc
-    each(n - 1, lambda d: pv_copy(d).start())
     fw_copy(half - 1, sibling).wait_recv()
     each(half - 1, lambda d: fw_copy(d, came_sibling(d)).wait_recv())
     each(half - 1, lambda d: ag_copy(d, me).wait_send())
@@ -356,13 +345,8 @@
             src_ref=st.at[1 - side, i], dst_ref=st.at[1 - side, i],
             send_sem=ex_send.at[v], recv_sem=ex_recv.at[v],
             device_id={"views": other}, device_id_type=MESH).wait_recv()
-    each(n - 1, lambda d: pv_copy(d).wait_recv())
-    total = pvbuf[0]
-    if n <= 16:
-        for d in range(n - 1):
-            total = total + pvbuf[d + 1]
-    else:
-        total = lax.fori_loop(1, n, lambda d, c: c + pvbuf[d], total)
+    each(everyone - 1, lambda d: pv_copy(d).wait_recv())
+    total = lax.fori_loop(1, everyone, lambda d, c: c + pvbuf[d], pvbuf[0], unroll=everyone <= 32)
     total = jnp.sum(total, axis=1, keepdims=True)
     power = [total[g:g + 1] + (total[GBAND + g - 1:GBAND + g] if g else 0.0) for g in range(GBAND)]
     power = [p / (rows_total * WIDE) + SHRINK_FLOOR for p in power]
@@ -377,8 +361,7 @@
             full[g, r] = factor * re
             if g:
                 full[GBAND + g - 1, r] = factor * im
-    each(nr - 1, lambda d: pw_copy(d).wait_send())
-    each(n - 1, lambda d: pv_copy(d).wait_send())
+    each(everyone - 1, lambda d: pv_copy(d).wait_send())
 
     cos, sin = twist_ref[0], twist_ref[1]
     first = first_ref[...]
@@ -456,8 +439,7 @@
             pltpu.VMEM((half - 1, strip, LANES), jnp.float32),
             pltpu.VMEM((n, strip, LANES), jnp.float32),
             pltpu.VMEM((NCOEF, 2, 2 * blocks, LANES), jnp.float32),
-            pltpu.VMEM((nr, SLOT, LANES), jnp.float32),
-            pltpu.VMEM((n, SLOT, LANES), jnp.float32),
+            pltpu.VMEM((n * nr, SLOT, LANES), jnp.float32),
             pltpu.VMEM((half, piece * SLOT, LANES), jnp.float32),
             pltpu.VMEM((paired * 2 * PAD, 2 * LANES), jnp.float32),
             pltpu.VMEM((2, paired * blocks, 3 * LANES), jnp.bfloat16),
@@ -466,8 +448,7 @@
             dma((half - 1,)), dma((half - 1,)),
             dma((half - 1,)), dma((half - 1,)),
             dma((half,)), dma((half,)),
-            dma((nr - 1,)), dma((nr - 1,)),
-            dma((n - 1,)), dma((n - 1,)),
+            dma((n * nr - 1,)), dma((n * nr - 1,)),
             dma((2 * (lap // piece),)), dma((half,)),
         ],
         compiler_params=pltpu.CompilerParams(

time: 24.7 us -> 25.4 us (1.028)
  Pallas kernels: 22.2 us -> 22.9 us
    pallas_call x1, Pallas kernels: 22.2 us -> 22.9 us  [on_device(): pl.pallas_call(functools.partial(kernel, n, nr, views, blocks, row_dev *...]
where the time goes in v3:
time: 25.4 us; the launch traced here: 25.2 us
  Pallas kernels  22.9 us (90%)
  local copies, waits for them, and re-layouts  2.33 us (9%)
    pallas_call x1, Pallas kernels, on_device(): pl.pallas_call(functools.partial(kernel, n, nr, views, blocks, row_dev *...  22.9 us
    reshape x2, local copies, waits for them, and re-layouts, on_device(): return out.reshape(paired, 2, WIDE)  1.25 us
    reshape x1, local copies, waits for them, and re-layouts, on_device(): out = out.reshape(paired, TURNS, 2, LANES).transpose(0, 2, 1, 3)  1.09 us

profile of v3, /device:TPU:0, one launch (start us, length us, event | category | flops | bytes accessed | tf_op | source)
XLA Modules:
  0.0 25.2 jit_solution(11774650411816068313)
XLA Ops:
  0.0 22.9 %shard_map.109 = f32[960,128]{1,0:T(8,128)} custom-call(s32[64]{0:T(128)} %partner_hbm.1, s32[2,8]{1,0:T(2,128)} %geometry_hbm.1, f32[1024]{0:T(1024)} %constant.16.clone.band_hbm, f32[16,64,128]{2,1,0:T(8,128)} %bitcast.13, bf16[2,128,384]{2,1,0:T(8,128)(2,1)} %constant.17.clone.phase_hbm, bf16[64,192]{1,0:T(8,128)(2,1)} %constant.18.clone.first_hbm, ...), custom_call_target="tpu_custom_call" | custom-call | flops 1000000000 | bytes 2000000 | tf_op jit(solution)/shard_map/pallas_call | solution.py:425
  22.9 1.1 %copy.18 = f32[8,60,2,128]{3,1,0,2:T(8,128)S(1)} copy(f32[8,60,2,128]{3,2,1,0:T(2,128)} %bitcast.12) | data formatting | bytes 983040 | tf_op jit(solution)/shard_map/reshape | solution.py:458
  24.0 0.1 reshape.15
  24.1 1.2 %copy.16 = f32[8,2,7680]{2,1,0:T(2,128)} copy(f32[8,2,7680]{2,0,1:T(8,128)S(1)} %reshape.15) | data formatting | bytes 983040 | tf_op jit(solution)/shard_map/reshape | solution.py:459

commit v4 on v2

--- a/solution.py
+++ b/solution.py
@@ -7,6 +7,7 @@
 from jax import lax
 from jax.experimental import pallas as pl
 from jax.experimental.pallas import tpu as pltpu
+from jax.experimental.layout import Layout, with_layout_constraint
 from jax.sharding import PartitionSpec as P
 
 GBAND = 4
@@ -251,7 +252,7 @@
         for m in range(len(pieces)):
             lap_copy(m, me).start()
 
-    for v in range(paired):
+    for v in range(paired // 2):
         ex_copy(v).start()
     agbuf[me] = cbuf[pl.ds(pl.multiple_of(s * strip, 8), strip), :]
 
@@ -317,6 +318,8 @@
         acc = acc + mine[q * SLOT:(q + 1) * SLOT]
     pwbuf[0] = acc
     each(nr - 1, lambda d: pw_copy(d).start())
+    for v in range(paired // 2, paired):
+        ex_copy(v).start()
     each(half - 1, lambda d: rs_copy(d).wait_send())
 
     @pl.when(jnp.logical_not(upper))
@@ -475,6 +478,7 @@
         cost_estimate=pl.CostEstimate(flops=10**9, bytes_accessed=2 * 10**6, transcendentals=131072),
     )(partner, geometry, band, x, *[jnp.asarray(t) for t in tables])
     out = out.reshape(paired, TURNS, 2, LANES).transpose(0, 2, 1, 3)
+    out = with_layout_constraint(out, Layout(major_to_minor=(0, 2, 1, 3)))
     return out.reshape(paired, 2, WIDE)
 
 

time: 24.7 us -> 23.3 us (0.943)
  Pallas kernels: 22.2 us -> 21.2 us
  local copies, waits for them, and re-layouts: 2.33 us -> 1.84 us
    reshape x3 -> x0, local copies, waits for them, and re-layouts: 2.33 us -> none  [the longest x2 1.25 us: on_device(): return out.reshape(paired, 2, WIDE)]
    unnamed x0 -> x1, local copies, waits for them, and re-layouts: none -> 1.84 us
    pallas_call x1, Pallas kernels: 22.2 us -> 21.2 us  [on_device(): pl.pallas_call(functools.partial(kernel, n, nr, views, blocks, row_dev *...]
where the time goes in v4:
time: 23.3 us; the launch traced here: 23.1 us
  Pallas kernels  21.2 us (91%)
  local copies, waits for them, and re-layouts  1.84 us (8%)
    pallas_call x1, Pallas kernels, on_device(): pl.pallas_call(functools.partial(kernel, n, nr, views, blocks, row_dev *...  21.2 us
    unnamed x1, local copies, waits for them, and re-layouts  1.84 us

profile of v4, /device:TPU:0, one launch (start us, length us, event | category | flops | bytes accessed | tf_op | source)
XLA Modules:
  0.0 23.1 jit_solution(2465052738126252566)
XLA Ops:
  0.0 21.2 %shard_map.109 = f32[960,128]{1,0:T(8,128)} custom-call(s32[64]{0:T(128)} %partner_hbm.1, s32[2,8]{1,0:T(2,128)} %geometry_hbm.1, f32[1024]{0:T(1024)} %constant.16.clone.band_hbm, f32[16,64,128]{2,1,0:T(8,128)} %bitcast.11, bf16[2,128,384]{2,1,0:T(8,128)(2,1)} %constant.17.clone.phase_hbm, bf16[64,192]{1,0:T(8,128)(2,1)} %constant.18.clone.first_hbm, ...), custom_call_target="tpu_custom_call" | custom-call | flops 1000000000 | bytes 2000000 | tf_op jit(solution)/shard_map/pallas_call | solution.py:445
  21.2 1.8 %copy.14 = f32[8,2,7680]{2,1,0:T(2,128)} copy(f32[8,2,7680]{2,1,0:T(2,128)} %bitcast.10) | data formatting | bytes 983040
